TPU v7x, 32 devices: a whole 2x2x4 slice. The times are simulated.
32 devices in a mesh: prow: 8 (over z, x), pcol: 4 (over y, core).
Axes of the slice: x: 2, y: 2, z: 4, core: 2. Of those that a mesh axis runs over, the one named last changes fastest.
Arguments:
- separator_inverse: float32 [12288, 12288], P('prow', 'pcol'), may hold values from -6 to 6
- panel: float32 [12288, 2048], P('pcol', 'prow'), may hold values from -0.0546875 to 0.0546875
- block_rows: int32 [16], replicated, may hold values 0 or 1
- pivot_inverse: float32 [2048, 2048], P('prow', 'pcol'), may hold values from -4 to 4
Outputs:
- off_diagonal: float32 [12288, 2048], P('prow', 'pcol')
- child_inverse: float32 [2048, 2048], P('prow', 'pcol')
All inputs are finite; a program needn't handle non-finite values.
Results may differ from a plain program's by a relative error of at most 0.000088.
Values sent between devices are 32-bit elements; how exact they have to be, the bound alone decides.
A program may use at most 128 MiB of HBM per device.

v0:
```python
import jax
import jax.numpy as jnp
from jax import lax
from jax.sharding import PartitionSpec as P

BS = 768


def from_root(value, axis, source):
    kept = jnp.where(lax.axis_index(axis) == source, value, 0).astype(value.dtype)
    return lax.psum(kept, axis)


def local(separator_inverse, panel, block_rows, pivot_inverse):
    local_rows = separator_inverse.shape[0]
    local_cols = separator_inverse.shape[1]
    row_index = lax.axis_index("prow")
    col_index = lax.axis_index("pcol")
    row_blocks = local_rows // BS
    col_blocks = local_cols // BS
    col_keep = lax.dynamic_slice_in_dim(block_rows, col_index * col_blocks, col_blocks).astype(
        jnp.float32
    )
    masked = (panel.reshape(col_blocks, BS, panel.shape[1]) * col_keep[:, None, None]).reshape(
        panel.shape
    )
    whole_panel = lax.all_gather(masked, "prow", axis=1, tiled=True)
    child_width = whole_panel.shape[1]
    share = child_width // lax.axis_size("pcol")
    part = lax.psum_scatter(
        lax.dot_general(
            whole_panel,
            separator_inverse,
            (((0,), (1,)), ((), ())),
            precision=lax.Precision.HIGHEST,
            preferred_element_type=jnp.float32,
        ),
        "pcol",
        scatter_dimension=0,
        tiled=True,
    )
    offset = row_index * local_rows - col_index * local_cols
    source = lax.dynamic_slice_in_dim(whole_panel, offset, local_rows, 0)
    root = row_index * lax.axis_size("pcol") // lax.axis_size("prow")
    panel_piece = from_root(source, "pcol", root)
    row_keep = lax.dynamic_slice_in_dim(block_rows, row_index * row_blocks, row_blocks).astype(
        jnp.float32
    )
    kept = (part.reshape(share, row_blocks, BS) * row_keep[None, :, None]).reshape(
        share, local_rows
    )
    off_diagonal = -kept.T
    gram_part = lax.dot_general(
        panel_piece,
        kept,
        (((0,), (1,)), ((), ())),
        precision=lax.Precision.HIGHEST,
        preferred_element_type=jnp.float32,
    )
    gram_share = lax.psum_scatter(gram_part, "prow", scatter_dimension=0, tiled=True)
    child_inverse = pivot_inverse + gram_share
    return (off_diagonal, child_inverse)


def solution(mesh):
    in_specs = (P("prow", "pcol"), P("pcol", "prow"), P(), P("prow", "pcol"))
    out_specs = (P("prow", "pcol"), P("prow", "pcol"))
    return jax.shard_map(local, mesh=mesh, in_specs=in_specs, out_specs=out_specs, check_vma=False)
```

profile of v0, /device:TPU:0, one launch (start us, length us, event | category | flops | bytes accessed | tf_op | source)
XLA Modules:
  0.0 988.5 jit_solution(2708385523220584284)
XLA Ops:
  7.2 0.0 all-gather.2.cloned.1.call-start
  7.2 0.7 dynamic-slice_convert_fusion.1
  7.9 0.1 mul.42
  8.0 4.0 broadcast_multiply_fusion
  12.1 0.0 all-gather.2.cloned.1.call-update
  12.1 0.0 all-reduce.2.cloned.1.call-start
  12.2 483.2 %all-gather.2.cloned.1.call-done = f32[3072,2048]{1,0:T(8,128)} async-done(((f32[3072,256]{1,0:T(8,128)}), f32[3072,2048]{1,0:T(8,128)}) %all-gather.2.cloned.1.call-update) | async-done | bytes 25165840 | tf_op jit(solution)/shard_map/all_gather | solution.py:27
  495.4 11.7 %dynamic-slice_select_fusion = f32[1536,2048]{1,0:T(8,128)} fusion(f32[3072,2048]{1,0:T(8,128)} %all-gather.2.cloned.1.call-done, s32[]{:T(128)S(6)} %select_n.26, pred[]{:T(512)S(6)} %eq.3), kind=kLoop, calls=%fused_computation | loop fusion | flops 3145728 | bytes 25165828 | tf_op jit(solution)/shard_map/jit(_where)/select_n | solution.py:10
  507.1 0.0 all-reduce.2.cloned.1.call-update
  507.1 0.0 reduce-scatter.3.cloned.1.call-start
  507.2 241.7 %fusion.3 = f32[2048,1536]{1,0:T(8,128)} fusion(f32[3072,2048]{1,0:T(8,128)} %all-gather.2.cloned.1.call-done, f32[1536,3072]{1,0:T(8,128)} %param.4), kind=kOutput, calls=%fused_computation.8 | convolution fusion | flops 115964116992 | bytes 56623104 | tf_op jit(solution)/shard_map/dot_general | solution.py:31
  748.9 0.0 copy-start
  748.9 0.0 reduce-scatter.3.cloned.1.call-update
  748.9 0.0 reduce-scatter.5.cloned.1.call-start
  749.0 0.6 copy-done
  749.6 0.1 dynamic-slice_convert_fusion
  749.6 0.1 mul.47
  749.7 0.0 all-reduce.2.cloned.1.call-done
  749.8 98.4 %reduce-scatter.3.cloned.1.call-done = f32[512,1536]{1,0:T(8,128)} async-done(((f32[2048,1536]{1,0:T(8,128)}), f32[512,1536]{1,0:T(8,128)}) %reduce-scatter.3.cloned.1.call-update) | async-done | bytes 3145744 | tf_op jit(solution)/shard_map/reduce_scatter | solution.py:30
  848.1 43.7 %fusion = f32[2048,512]{1,0:T(8,128)} fusion(f32[1536,2048]{1,0:T(8,128)} %all-reduce.2.cloned.1.call-done, f32[512,1536]{1,0:T(8,128)} %reduce-scatter.3.cloned.1.call-done, f32[1536]{0:T(1024)S(1)} %mul.48), kind=kOutput, calls=%fused_computation.2 | convolution fusion | flops 19328139264 | bytes 19929088 | tf_op jit(solution)/shard_map/dot_general | solution.py:53
  891.8 0.0 reduce-scatter.5.cloned.1.call-update
  891.8 2.2 negate_bitcast_fusion
  894.1 2.4 copy.6
  896.5 83.4 %reduce-scatter.5.cloned.1.call-done = f32[256,512]{1,0:T(8,128)} async-done(((f32[2048,512]{1,0:T(8,128)}), f32[256,512]{1,0:T(8,128)}) %reduce-scatter.5.cloned.1.call-update) | async-done | bytes 524304 | tf_op jit(solution)/shard_map/reduce_scatter | solution.py:60
  979.9 2.1 add.22
  (2 shorter events, 0.0 us)
Async XLA Ops:
  7.2 488.2 %all-gather.2.cloned.1.call-start = ((), (), s32[]{:S(2)}) async-start(), calls=%async_computation.2 | async-start | bytes 28311552 | tf_op jit(solution)/shard_map/all_gather | solution.py:27
  12.1 737.7 %all-reduce.2.cloned.1.call-start = ((), (), s32[]{:S(2)}) async-start(), calls=%async_computation.4 | async-start | bytes 25165824 | tf_op jit(solution)/shard_map/psum | solution.py:11
  507.1 341.0 %reduce-scatter.3.cloned.1.call-start = ((), (), s32[]{:S(2)}) async-start(), calls=%async_computation.3 | async-start | bytes 15728640 | tf_op jit(solution)/shard_map/reduce_scatter | solution.py:30
  748.9 0.7 copy-start
  748.9 231.0 %reduce-scatter.5.cloned.1.call-start = ((), (), s32[]{:S(2)}) async-start(), calls=%async_computation.5 | async-start | bytes 4718592 | tf_op jit(solution)/shard_map/reduce_scatter | solution.py:60
Sparse Core Ops, SparseCore 0:
  12.2 483.1 all-gather.1
  507.3 220.6 all-reduce.1
  749.1 99.0 reduce-scatter.2
  892.0 87.8 reduce-scatter.4
where the time goes:
time: 989 us
  waiting for transfers between devices  665 us (67%)
  matrix products  285 us (29%)
  other arithmetic  20.9 us (2%)
  between operations  13.8 us (1%)
    all_gather x1, waiting for transfers between devices, local(): whole_panel = lax.all_gather(masked, 'prow', axis=1, tiled=True)  483 us
    dot_general x1, matrix products, local(): lax.dot_general(whole_panel, separator_inverse, (((0,), (1,)), ((), ())),...  242 us
    reduce_scatter x1, waiting for transfers between devices, local(): lax.psum_scatter(lax.dot_general(whole_panel, separator_inverse, (((0,),...  98.4 us
    reduce_scatter x1, waiting for transfers between devices, local(): lax.psum_scatter(gram_part, 'prow', scatter_dimension=0, tiled=True)  83.4 us
    dot_general x1, matrix products, local(): lax.dot_general(panel_piece, kept, (((0,), (1,)), ((), ())), precision=la...  43.7 us
  transfers between devices with their start and end apart: 4, of which 3 were waited for; matrix products, arithmetic and copies ran while one was open for 25% of the time, Pallas kernels for 0%

commit v1 on v0

v1 whole, which is shorter than its diff:
```python
import functools

import jax
import jax.numpy as jnp
from jax import lax
from jax.experimental import pallas as pl
from jax.experimental.pallas import tpu as pltpu
from jax.sharding import PartitionSpec as P

BS = 768
PIECES = 2
STRIP = 64
TILE_ROWS = 512
TILE_DEPTH = 1024
VMEM_BYTES = 62 * 1024 * 1024
MESH = pl.DeviceIdType.MESH


def product(left, right, dims):
    return lax.dot_general(
        left,
        right,
        (dims, ((), ())),
        precision=lax.Precision.HIGH,
        preferred_element_type=jnp.float32,
    )


def spread(value, root, row_index, col_index, rows, cols):
    held = jnp.where(col_index == root, value, 0)
    done = 0
    bit = cols // 2
    while bit:
        pairs = []
        for r in range(rows):
            start = r * cols // rows
            for c in range(cols):
                if (c ^ start) & ~done == 0:
                    pairs.append((r * cols + c, r * cols + (c ^ bit)))
        held = held + lax.ppermute(held, ("prow", "pcol"), pairs)
        done |= bit
        bit //= 2
    return held


def local(separator_inverse, panel, block_rows, pivot_inverse):
    local_rows, local_cols = separator_inverse.shape
    rows, cols = lax.axis_size("prow"), lax.axis_size("pcol")
    row_index, col_index = lax.axis_index("prow"), lax.axis_index("pcol")
    row_blocks, col_blocks = local_rows // BS, local_cols // BS
    col_keep = lax.dynamic_slice_in_dim(block_rows, col_index * col_blocks, col_blocks)
    row_keep = lax.dynamic_slice_in_dim(block_rows, row_index * row_blocks, row_blocks)
    col_keep = jnp.repeat(col_keep.astype(jnp.float32), BS)
    row_keep = jnp.repeat(row_keep.astype(jnp.float32), BS)
    masked = panel * col_keep[:, None]
    width = panel.shape[1]
    piece = max(width // PIECES, 128)
    pieces = width // piece
    group = rows // cols
    offset = row_index * local_rows - col_index * local_cols
    root = row_index * cols // rows
    lefts, rights = [], []
    for g in range(pieces):
        whole = lax.all_gather(masked[:, g * piece : (g + 1) * piece], "prow", axis=1, tiled=True)
        source = lax.dynamic_slice_in_dim(whole, offset, local_rows, 0)
        lefts.append(spread(source, root, row_index, col_index, rows, cols))
        part = product(whole, separator_inverse, ((0,), (1,)))
        share = lax.psum_scatter(part, "pcol", scatter_dimension=0, tiled=True)
        rights.append(share * row_keep[None, :])
    kept = jnp.stack([v.reshape(group, piece, local_rows) for v in rights], axis=1)
    kept = kept.reshape(group * width, local_rows)
    left = jnp.stack([v.reshape(local_rows, rows, piece) for v in lefts], axis=2)
    left = left.reshape(local_rows, rows * width)
    gram_part = product(left, kept, ((0,), (1,)))
    gram_share = lax.psum_scatter(gram_part, "prow", scatter_dimension=0, tiled=True)
    return (-kept.T, pivot_inverse + gram_share)


def device_kernel(geometry, sep_ref, panel_ref, colmask_ref, rowmask_ref, off_ref, mr_ref,
                  s_hi, s_lo, m_buf, m_hi, m_lo, p_buf, near, far,
                  load_sem, own_sem, gather_send, gather_recv, p_send, near_recv,
                  far_send, far_recv, root_send, root_recv, root_own, out_sem):
    rows, cols, span = geometry
    local_rows, local_cols = s_hi.shape
    width = m_buf.shape[2]
    r, c = lax.axis_index("prow"), lax.axis_index("pcol")
    z, x = r // 2, lax.rem(r, 2)
    y, core = c // 2, lax.rem(c, 2)
    across = (z * 2 + 1 - x, c)
    above, below = (r + 2, c), (r - 2, c)
    mate = (r, y * 2 + 1 - core)
    other = (r, (1 - y) * 2 + core)
    has_above, has_below = z < span - 1, z > 0
    is_root = c == z
    is_relay = c == lax.rem(z + 2, 4)

    own = pltpu.make_async_copy(panel_ref, m_buf.at[r], own_sem)
    own.start()

    def tile(i):
        return pltpu.make_async_copy(
            sep_ref.at[:, pl.ds(pl.multiple_of(i * width, width), width)],
            p_buf.at[lax.rem(i, 2)], load_sem.at[lax.rem(i, 2)])

    tile(0).start()

    barrier = pltpu.get_barrier_semaphore()
    for peer in (across, mate, other):
        pl.semaphore_signal(barrier, inc=1, device_id=peer, device_id_type=MESH)

    @pl.when(has_above)
    def _():
        pl.semaphore_signal(barrier, inc=1, device_id=above, device_id_type=MESH)

    @pl.when(has_below)
    def _():
        pl.semaphore_signal(barrier, inc=1, device_id=below, device_id_type=MESH)

    pl.semaphore_wait(barrier, 3 + has_above.astype(jnp.int32) + has_below.astype(jnp.int32))

    def place(k):
        partner = jnp.logical_or(jnp.logical_and(k >= 2, lax.rem(k, 2) == 0), k == 7)
        j = jnp.where(partner, jnp.where(k == 7, 3, (k - 2) // 2), (k + 1) // 2)
        inner = jnp.logical_and(z > 0, z < span - 1)
        q = jnp.where(jnp.logical_and(inner, j < 2), 1 - j, j)
        source_z = jnp.where(z < 2, q, span - 1 - q)
        return source_z * 2 + jnp.where(partner, 1 - x, x), source_z, partner

    def gather(slot, way, target):
        return pltpu.make_async_remote_copy(
            src_ref=m_buf.at[slot], dst_ref=m_buf.at[slot],
            send_sem=gather_send.at[way, slot], recv_sem=gather_recv.at[slot],
            device_id=target, device_id_type=MESH)

    def forwards(slot, source_z, partner, act):
        line = jnp.logical_not(partner)

        @pl.when(line)
        def _():
            act(gather(slot, 0, across))

        @pl.when(jnp.logical_and(line, jnp.logical_and(source_z <= z, has_above)))
        def _():
            act(gather(slot, 1, above))

        @pl.when(jnp.logical_and(line, jnp.logical_and(source_z >= z, has_below)))
        def _():
            act(gather(slot, 2, below))

    def to_mate(slot):
        return pltpu.make_async_remote_copy(
            src_ref=m_buf.at[slot, pl.ds(pl.multiple_of(x * local_rows, local_rows), local_rows)],
            dst_ref=mr_ref.at[slot], send_sem=root_send.at[0, slot], recv_sem=root_recv.at[slot],
            device_id=mate, device_id_type=MESH)

    def to_other(slot):
        return pltpu.make_async_remote_copy(
            src_ref=m_buf.at[slot, pl.ds(pl.multiple_of(x * local_rows, local_rows), local_rows)],
            dst_ref=mr_ref.at[slot], send_sem=root_send.at[1, slot], recv_sem=root_recv.at[slot],
            device_id=other, device_id_type=MESH)

    def relay(slot):
        return pltpu.make_async_remote_copy(
            src_ref=mr_ref.at[slot], dst_ref=mr_ref.at[slot],
            send_sem=root_send.at[0, slot], recv_sem=root_recv.at[slot],
            device_id=mate, device_id_type=MESH)

    def keep_own(slot):
        return pltpu.make_async_copy(
            m_buf.at[slot, pl.ds(pl.multiple_of(x * local_rows, local_rows), local_rows)],
            mr_ref.at[slot], root_own.at[slot])

    def partial(slot):
        i = (slot // 4) * 2 + lax.rem(slot, 2)
        return pltpu.make_async_remote_copy(
            src_ref=p_buf.at[0], dst_ref=near.at[i], send_sem=p_send, recv_sem=near_recv.at[i],
            device_id=mate, device_id_type=MESH)

    def chip_sum(slot):
        b = lax.rem(slot, 2)
        return pltpu.make_async_remote_copy(
            src_ref=near.at[(slot // 4) * 2 + b], dst_ref=far.at[b],
            send_sem=far_send.at[b], recv_sem=far_recv.at[b],
            device_id=other, device_id_type=MESH)

    def core_of(slot):
        return lax.rem(slot // 2, 2)

    own.wait()
    forwards(r, z, jnp.bool_(False), lambda copy: copy.start())

    tiles = local_cols // width

    def split(i, carry):
        @pl.when(i + 1 < tiles)
        def _():
            tile(i + 1).start()

        tile(i).wait()
        columns = pl.ds(pl.multiple_of(i * width, width), width)

        def strip(t, inner):
            part = pl.ds(pl.multiple_of(t * STRIP, STRIP), STRIP)
            value = p_buf[lax.rem(i, 2), part, :] * colmask_ref[:, columns] * rowmask_ref[part, :]
            high = value.astype(jnp.bfloat16)
            s_hi[part, columns] = high
            s_lo[part, columns] = (value - high.astype(jnp.float32)).astype(jnp.bfloat16)
            return inner

        return lax.fori_loop(0, local_rows // STRIP, strip, carry)

    lax.fori_loop(0, tiles, split, 0)

    def relay_at(k):
        slot, _, _ = place(k)

        @pl.when(is_relay)
        def _():
            relay(slot).wait_recv()
            relay(slot).start()

    def step(k, carry):
        slot, source_z, partner = place(k)

        @pl.when(k > 0)
        def _():
            gather(slot, 0, across).wait_recv()
            forwards(slot, source_z, partner, lambda copy: copy.start())

        @pl.when(is_root)
        def _():
            to_other(slot).start()
            to_mate(slot).start()
            keep_own(slot).start()

        @pl.when(k > 0)
        def _():
            before, _, _ = place(k - 1)

            @pl.when(core_of(before) != core)
            def _():
                partial(before).wait_send()

        def cut(t, inner):
            part = pl.ds(pl.multiple_of(t * STRIP, STRIP), STRIP)
            value = m_buf[slot, part, :]
            high = value.astype(jnp.bfloat16)
            m_hi[part, :] = high
            m_lo[part, :] = (value - high.astype(jnp.float32)).astype(jnp.bfloat16)
            return inner

        lax.fori_loop(0, local_cols // STRIP, cut, 0)

        def multiply(t, inner):
            part = pl.ds(pl.multiple_of(t * TILE_ROWS, TILE_ROWS), TILE_ROWS)
            total = None
            for d in range(local_cols // TILE_DEPTH):
                depth = pl.ds(d * TILE_DEPTH, TILE_DEPTH)
                a, b = s_hi[part, depth], s_lo[part, depth]
                u, v = m_hi[depth, :], m_lo[depth, :]
                term = (jnp.dot(a, u, preferred_element_type=jnp.float32)
                        + jnp.dot(a, v, preferred_element_type=jnp.float32)
                        + jnp.dot(b, u, preferred_element_type=jnp.float32))
                total = term if total is None else total + term
            p_buf[0, part, :] = total
            return inner

        lax.fori_loop(0, local_rows // TILE_ROWS, multiply, 0)

        @pl.when(core_of(slot) != core)
        def _():
            partial(slot).start()

        @pl.when(k > 0)
        def _():
            relay_at(k - 1)

        @pl.when(core_of(slot) == core)
        def _():
            partial(slot).wait_recv()
            i = (slot // 4) * 2 + lax.rem(slot, 2)

            def add(t, inner):
                part = pl.ds(pl.multiple_of(t * STRIP, STRIP), STRIP)
                near[i, part, :] += p_buf[0, part, :]
                return inner

            lax.fori_loop(0, local_rows // STRIP, add, 0)

            @pl.when(slot // 4 != y)
            def _():
                chip_sum(slot).start()

        return carry

    lax.fori_loop(0, rows, step, 0)

    last, _, _ = place(rows - 1)

    @pl.when(core_of(last) != core)
    def _():
        partial(last).wait_send()

    relay_at(rows - 1)

    def finish(b):
        return pltpu.make_async_copy(
            near.at[y * 2 + b], off_ref.at[:, pl.ds(b * width, width)], out_sem.at[b])

    for b in range(2):
        mine = c * 2 + b
        chip_sum(mine).wait_recv()

        def total(t, inner):
            part = pl.ds(pl.multiple_of(t * STRIP, STRIP), STRIP)
            near[y * 2 + b, part, :] += far[b, part, :]
            return inner

        lax.fori_loop(0, local_rows // STRIP, total, 0)
        finish(b).start()

    def drain(k, carry):
        slot, source_z, partner = place(k)
        forwards(slot, source_z, partner, lambda copy: copy.wait_send())

        @pl.when(is_root)
        def _():
            to_other(slot).wait_send()
            to_mate(slot).wait_send()
            keep_own(slot).wait()

        @pl.when(is_relay)
        def _():
            relay(slot).wait_send()

        @pl.when(jnp.logical_not(jnp.logical_or(is_root, is_relay)))
        def _():
            relay(slot).wait_recv()

        return carry

    lax.fori_loop(0, rows, drain, 0)
    for b in range(2):
        chip_sum((1 - y) * 4 + core * 2 + b).wait_send()
        finish(b).wait()


def fused(separator_inverse, panel, block_rows, pivot_inverse):
    local_rows, local_cols = separator_inverse.shape
    width = panel.shape[1]
    rows, cols = lax.axis_size("prow"), lax.axis_size("pcol")
    row_index, col_index = lax.axis_index("prow"), lax.axis_index("pcol")
    row_blocks, col_blocks = local_rows // BS, local_cols // BS
    col_keep = lax.dynamic_slice_in_dim(block_rows, col_index * col_blocks, col_blocks)
    row_keep = lax.dynamic_slice_in_dim(block_rows, row_index * row_blocks, row_blocks)
    col_mask = jnp.repeat(col_keep.astype(jnp.float32), BS)[None, :]
    row_mask = -jnp.repeat(row_keep.astype(jnp.float32), BS)[:, None]
    dma, f32, bf16 = pltpu.SemaphoreType.DMA, jnp.float32, jnp.bfloat16
    flops = 6 * local_rows * local_cols * rows * width
    off, source = pl.pallas_call(
        functools.partial(device_kernel, (rows, cols, rows // 2)),
        out_shape=(jax.ShapeDtypeStruct((local_rows, 2 * width), f32),
                   jax.ShapeDtypeStruct((rows, local_rows, width), f32)),
        in_specs=[pl.BlockSpec(memory_space=pl.ANY), pl.BlockSpec(memory_space=pl.ANY),
                  pl.BlockSpec(memory_space=pltpu.VMEM), pl.BlockSpec(memory_space=pltpu.VMEM)],
        out_specs=(pl.BlockSpec(memory_space=pl.ANY), pl.BlockSpec(memory_space=pl.ANY)),
        scratch_shapes=[
            pltpu.VMEM((local_rows, local_cols), bf16),
            pltpu.VMEM((local_rows, local_cols), bf16),
            pltpu.VMEM((rows, local_cols, width), f32),
            pltpu.VMEM((local_cols, width), bf16),
            pltpu.VMEM((local_cols, width), bf16),
            pltpu.VMEM((2, local_rows, width), f32),
            pltpu.VMEM((4, local_rows, width), f32),
            pltpu.VMEM((2, local_rows, width), f32),
            dma((2,)), dma, dma((3, rows)), dma((rows,)), dma, dma((4,)),
            dma((2,)), dma((2,)), dma((2, rows)), dma((rows,)), dma((rows,)), dma((2,)),
        ],
        compiler_params=pltpu.CompilerParams(
            collective_id=0, has_side_effects=True, vmem_limit_bytes=VMEM_BYTES),
        cost_estimate=pl.CostEstimate(
            flops=flops, bytes_accessed=4 * local_rows * local_cols, transcendentals=0),
    )(separator_inverse, panel, col_mask, row_mask)
    gram_part = product(source, off, ((1,), (0,))).reshape(rows * width, 2 * width)
    gram_share = lax.psum_scatter(gram_part, "prow", scatter_dimension=0, tiled=True)
    return (off, pivot_inverse - gram_share)


def solution(mesh):
    in_specs = (P("prow", "pcol"), P("pcol", "prow"), P(), P("prow", "pcol"))
    out_specs = (P("prow", "pcol"), P("prow", "pcol"))
    body = fused if (mesh.shape["prow"], mesh.shape["pcol"]) == (8, 4) else local
    return jax.shard_map(body, mesh=mesh, in_specs=in_specs, out_specs=out_specs, check_vma=False)
```

time: 989 us -> 460 us (0.47)
  waiting for transfers between devices: 665 us -> 102 us
  Pallas kernels: 0 us -> 321 us
  matrix products: 285 us -> 15.3 us
  other arithmetic: 20.9 us -> 3.53 us
    all_gather x1 -> x0, waiting for transfers between devices: 483 us -> none  [local(): whole_panel = lax.all_gather(masked, 'prow', axis=1, tiled=True)]
    pallas_call x0 -> x1, Pallas kernels: none -> 321 us  [fused(): pl.pallas_call(functools.partial(device_kernel, (rows, cols, rows // 2)),...]
    dot_general x2 -> x1, matrix products: 285 us -> 15.3 us  [product(): lax.dot_general(left, right, (dims, ((), ())), precision=lax.Precision.HI...]
    reduce_scatter x2 -> x1, waiting for transfers between devices: 182 us -> 102 us  [fused(): lax.psum_scatter(gram_part, 'prow', scatter_dimension=0, tiled=True)]
    select_n x1 -> x0, other arithmetic: 11.7 us -> none  [from_root(): jnp.where(lax.axis_index(axis) == source, value, 0).astype(value.dtype)]
  transfers between devices with their start and end apart: 4 -> 1, of which waited for: 3 -> 1; matrix products, arithmetic and copies ran while one was open for 25% -> 0% of each run, Pallas kernels for 0% -> 0%
where the time goes in v1:
time: 460 us
  Pallas kernels  321 us (70%)
  waiting for transfers between devices  102 us (22%)
  matrix products  15.3 us (3%)
  between operations  14 us (3%)
    pallas_call x1, Pallas kernels, fused(): pl.pallas_call(functools.partial(device_kernel, (rows, cols, rows // 2)),...  321 us
    reduce_scatter x1, waiting for transfers between devices, fused(): lax.psum_scatter(gram_part, 'prow', scatter_dimension=0, tiled=True)  102 us
    dot_general x1, matrix products, product(): lax.dot_general(left, right, (dims, ((), ())), precision=lax.Precision.HI...  15.3 us
  transfers between devices with their start and end apart: 1, of which 1 were waited for; matrix products, arithmetic and copies ran while one was open for 0% of the time, Pallas kernels for 0%

profile of v1, /device:TPU:0, one launch (start us, length us, event | category | flops | bytes accessed | tf_op | source)
XLA Modules:
  0.0 460.2 jit_solution(9128001716095735359)
XLA Ops:
  7.2 0.0 reduce-scatter.2.cloned.1.call-start
  7.2 0.7 convert_negate_fusion
  7.9 0.7 dynamic-slice_convert_fusion
  8.7 0.1 broadcast_bitcast_fusion.1
  8.8 0.1 broadcast_bitcast_fusion
  8.8 0.6 copy.10
  9.4 1.2 copy.12
  10.6 321.2 %shard_map.59 = (f32[1536,512]{1,0:T(8,128)}, f32[8,1536,256]{2,1,0:T(8,128)}) custom-call(f32[1536,3072]{1,0:T(8,128)} %sep_ref.1, f32[3072,256]{1,0:T(8,128)} %panel_ref.1, f32[1,3072]{1,0:T(1,128)} %bitcast.17, f32[1536,1]{1,0:T(8,128)} %bitcast.15), custom_call_target="tpu_custom_call" | custom-call | flops 57982058496 | bytes 18874368 | tf_op jit(solution)/shard_map/pallas_call | solution.py:360
  331.9 15.3 %fusion = f32[8,256,512]{2,1,0:T(8,128)} fusion(f32[8,1536,256]{2,1,0:T(8,128)} %get-tuple-element.5, f32[1536,512]{1,0:T(8,128)} %get-tuple-element.8), kind=kOutput, calls=%fused_computation | convolution fusion | flops 9663676416 | bytes 19922944 | tf_op jit(solution)/shard_map/dot_general | solution.py:20
  347.1 0.0 copy-start
  347.1 0.0 reduce-scatter.2.cloned.1.call-update
  347.2 102.4 %reduce-scatter.2.cloned.1.call-done = f32[256,512]{1,0:T(8,128)} async-done(((f32[2048,512]{1,0:T(8,128)}), f32[256,512]{1,0:T(8,128)}) %reduce-scatter.2.cloned.1.call-update) | async-done | bytes 524304 | tf_op jit(solution)/shard_map/reduce_scatter | solution.py:385
  449.6 2.1 sub.3
  451.7 0.0 copy-done
  451.7 1.7 copy.14
  (1 shorter events, 0.0 us)
Async XLA Ops:
  7.2 442.4 %reduce-scatter.2.cloned.1.call-start = ((), (), s32[]{:S(2)}) async-start(), calls=%async_computation.1 | async-start | bytes 4718592 | tf_op jit(solution)/shard_map/reduce_scatter | solution.py:385
  347.1 104.5 %copy-start = (f32[1536,512]{1,0:T(8,128)S(1)}, f32[1536,512]{1,0:T(8,128)}, u32[]{:S(2)}) copy-start(f32[1536,512]{1,0:T(8,128)} %get-tuple-element.8) | copy-start | bytes 9437188
Sparse Core Ops, SparseCore 0:
  347.3 102.2 reduce-scatter.1

commit v2 on v1

--- a/solution.py
+++ b/solution.py
@@ -12,6 +12,7 @@
 STRIP = 64
 TILE_ROWS = 512
 TILE_DEPTH = 1024
+EARLY = 2560
 VMEM_BYTES = 62 * 1024 * 1024
 MESH = pl.DeviceIdType.MESH
 
@@ -76,10 +77,12 @@
     return (-kept.T, pivot_inverse + gram_share)
 
 
-def device_kernel(geometry, sep_ref, panel_ref, colmask_ref, rowmask_ref, off_ref, mr_ref,
-                  s_hi, s_lo, m_buf, m_hi, m_lo, p_buf, near, far,
-                  load_sem, own_sem, gather_send, gather_recv, p_send, near_recv,
-                  far_send, far_recv, root_send, root_recv, root_own, out_sem):
+def device_kernel(geometry, sep_ref, panel_ref, colmask_ref, rowmask_ref, pivot_ref,
+                  off_ref, child_ref, mr_ref, gram_z,
+                  s_hi, s_lo, m_buf, m_hi, m_lo, p_buf, near, far, gram_x,
+                  load_sem, own_sem, gather_send, gather_recv, late_send, late_recv,
+                  p_send, near_recv, far_send, far_recv, root_send, root_recv, root_own, out_sem,
+                  rows_sem, x_send, x_recv, z_send, z_recv, pivot_sem, child_sem, stage_sem):
     rows, cols, span = geometry
     local_rows, local_cols = s_hi.shape
     width = m_buf.shape[2]
@@ -97,10 +100,13 @@
     own = pltpu.make_async_copy(panel_ref, m_buf.at[r], own_sem)
     own.start()
 
+    half = local_rows // 2
+
     def tile(i):
+        part = pl.ds(pl.multiple_of(lax.rem(i, 2) * half, half), half)
         return pltpu.make_async_copy(
-            sep_ref.at[:, pl.ds(pl.multiple_of(i * width, width), width)],
-            p_buf.at[lax.rem(i, 2)], load_sem.at[lax.rem(i, 2)])
+            sep_ref.at[part, pl.ds(pl.multiple_of((i // 2) * width, width), width)],
+            p_buf.at[part], load_sem.at[lax.rem(i, 2)])
 
     tile(0).start()
 
@@ -118,34 +124,68 @@
 
     pl.semaphore_wait(barrier, 3 + has_above.astype(jnp.int32) + has_below.astype(jnp.int32))
 
+    def line(j):
+        inner = jnp.logical_and(z > 0, z < span - 1)
+        q = jnp.where(jnp.logical_and(inner, j < 2), 1 - j, j)
+        return jnp.where(z < 2, q, span - 1 - q)
+
     def place(k):
         partner = jnp.logical_or(jnp.logical_and(k >= 2, lax.rem(k, 2) == 0), k == 7)
         j = jnp.where(partner, jnp.where(k == 7, 3, (k - 2) // 2), (k + 1) // 2)
-        inner = jnp.logical_and(z > 0, z < span - 1)
-        q = jnp.where(jnp.logical_and(inner, j < 2), 1 - j, j)
-        source_z = jnp.where(z < 2, q, span - 1 - q)
+        source_z = line(j)
         return source_z * 2 + jnp.where(partner, 1 - x, x), source_z, partner
 
     def gather(slot, way, target):
-        return pltpu.make_async_remote_copy(
-            src_ref=m_buf.at[slot], dst_ref=m_buf.at[slot],
+        part = pl.ds(0, EARLY)
+        return pltpu.make_async_remote_copy(
+            src_ref=m_buf.at[slot, part], dst_ref=m_buf.at[slot, part],
             send_sem=gather_send.at[way, slot], recv_sem=gather_recv.at[slot],
             device_id=target, device_id_type=MESH)
 
+    def gather_late(slot, way, target):
+        part = pl.ds(EARLY, local_cols - EARLY)
+        return pltpu.make_async_remote_copy(
+            src_ref=m_buf.at[slot, part], dst_ref=m_buf.at[slot, part],
+            send_sem=late_send.at[way, slot], recv_sem=late_recv.at[slot],
+            device_id=target, device_id_type=MESH)
+
+    def goes_up(source_z):
+        return jnp.logical_and(source_z <= z, has_above)
+
+    def goes_down(source_z):
+        return jnp.logical_and(source_z >= z, has_below)
+
+    def along(copy, slot, source_z, act):
+        @pl.when(goes_up(source_z))
+        def _():
+            act(copy(slot, 1, above))
+
+        @pl.when(goes_down(source_z))
+        def _():
+            act(copy(slot, 2, below))
+
     def forwards(slot, source_z, partner, act):
-        line = jnp.logical_not(partner)
-
-        @pl.when(line)
-        def _():
+        @pl.when(jnp.logical_not(partner))
+        def _():
+            @pl.when(source_z == z)
+            def _():
+                act(gather_late(slot, 0, across))
+
+            along(gather_late, slot, source_z, act)
+            along(gather, slot, source_z, act)
             act(gather(slot, 0, across))
 
-        @pl.when(jnp.logical_and(line, jnp.logical_and(source_z <= z, has_above)))
-        def _():
-            act(gather(slot, 1, above))
-
-        @pl.when(jnp.logical_and(line, jnp.logical_and(source_z >= z, has_below)))
-        def _():
-            act(gather(slot, 2, below))
+    def passes_on(source_z):
+        return jnp.logical_or(goes_up(source_z), goes_down(source_z))
+
+    def pass_on(j):
+        source_z = line(j)
+        slot = source_z * 2 + 1 - x
+
+        @pl.when(passes_on(source_z))
+        def _():
+            gather_late(slot, 0, across).wait_recv()
+            along(gather_late, slot, source_z, lambda copy: copy.start())
 
     def to_mate(slot):
         return pltpu.make_async_remote_copy(
@@ -173,7 +213,7 @@
     def partial(slot):
         i = (slot // 4) * 2 + lax.rem(slot, 2)
         return pltpu.make_async_remote_copy(
-            src_ref=p_buf.at[0], dst_ref=near.at[i], send_sem=p_send, recv_sem=near_recv.at[i],
+            src_ref=p_buf, dst_ref=near.at[i], send_sem=p_send, recv_sem=near_recv.at[i],
             device_id=mate, device_id_type=MESH)
 
     def chip_sum(slot):
@@ -189,7 +229,7 @@
     own.wait()
     forwards(r, z, jnp.bool_(False), lambda copy: copy.start())
 
-    tiles = local_cols // width
+    tiles = 2 * (local_cols // width)
 
     def split(i, carry):
         @pl.when(i + 1 < tiles)
@@ -197,17 +237,17 @@
             tile(i + 1).start()
 
         tile(i).wait()
-        columns = pl.ds(pl.multiple_of(i * width, width), width)
+        columns = pl.ds(pl.multiple_of((i // 2) * width, width), width)
 
         def strip(t, inner):
-            part = pl.ds(pl.multiple_of(t * STRIP, STRIP), STRIP)
-            value = p_buf[lax.rem(i, 2), part, :] * colmask_ref[:, columns] * rowmask_ref[part, :]
+            part = pl.ds(pl.multiple_of(lax.rem(i, 2) * half + t * STRIP, STRIP), STRIP)
+            value = p_buf[part, :] * colmask_ref[:, columns] * rowmask_ref[(lax.rem(i, 2) * half + t * STRIP) // BS]
             high = value.astype(jnp.bfloat16)
             s_hi[part, columns] = high
             s_lo[part, columns] = (value - high.astype(jnp.float32)).astype(jnp.bfloat16)
             return inner
 
-        return lax.fori_loop(0, local_rows // STRIP, strip, carry)
+        return lax.fori_loop(0, half // STRIP, strip, carry)
 
     lax.fori_loop(0, tiles, split, 0)
 
@@ -225,7 +265,17 @@
         @pl.when(k > 0)
         def _():
             gather(slot, 0, across).wait_recv()
+
+            @pl.when(jnp.logical_not(jnp.logical_and(partner, passes_on(source_z))))
+            def _():
+                gather_late(slot, 0, across).wait_recv()
+
             forwards(slot, source_z, partner, lambda copy: copy.start())
+
+        for turn, j in ((1, 0), (3, 1), (5, 2), (5, 3)):
+            @pl.when(k == turn)
+            def _():
+                pass_on(j)
 
         @pl.when(is_root)
         def _():
@@ -262,7 +312,7 @@
                         + jnp.dot(a, v, preferred_element_type=jnp.float32)
                         + jnp.dot(b, u, preferred_element_type=jnp.float32))
                 total = term if total is None else total + term
-            p_buf[0, part, :] = total
+            p_buf[part, :] = total
             return inner
 
         lax.fori_loop(0, local_rows // TILE_ROWS, multiply, 0)
@@ -282,7 +332,7 @@
 
             def add(t, inner):
                 part = pl.ds(pl.multiple_of(t * STRIP, STRIP), STRIP)
-                near[i, part, :] += p_buf[0, part, :]
+                near[i, part, :] += p_buf[part, :]
                 return inner
 
             lax.fori_loop(0, local_rows // STRIP, add, 0)
@@ -303,46 +353,213 @@
 
     relay_at(rows - 1)
 
+    def own_rows(k):
+        slot, _, _ = place(k)
+        return pltpu.make_async_copy(
+            mr_ref.at[slot], m_buf.at[slot, pl.ds(0, local_rows)], rows_sem.at[slot])
+
+    def drain(k, carry):
+        slot, source_z, partner = place(k)
+        forwards(slot, source_z, partner, lambda copy: copy.wait_send())
+
+        @pl.when(partner)
+        def _():
+            along(gather_late, slot, source_z, lambda copy: copy.wait_send())
+
+        @pl.when(is_root)
+        def _():
+            to_other(slot).wait_send()
+            to_mate(slot).wait_send()
+            keep_own(slot).wait()
+
+        @pl.when(is_relay)
+        def _():
+            relay(slot).wait_send()
+
+        @pl.when(jnp.logical_not(jnp.logical_or(is_root, is_relay)))
+        def _():
+            relay(slot).wait_recv()
+
+        own_rows(k).start()
+        return carry
+
+    lax.fori_loop(0, rows, drain, 0)
+
+    def pivot(b):
+        return pltpu.make_async_copy(
+            pivot_ref.at[:, pl.ds(b * width, width)],
+            m_buf.at[0, pl.ds(local_rows + 2 * width + b * width, width)], pivot_sem.at[b])
+
     def finish(b):
         return pltpu.make_async_copy(
             near.at[y * 2 + b], off_ref.at[:, pl.ds(b * width, width)], out_sem.at[b])
 
     for b in range(2):
+        pivot(b).start()
         mine = c * 2 + b
         chip_sum(mine).wait_recv()
 
         def total(t, inner):
             part = pl.ds(pl.multiple_of(t * STRIP, STRIP), STRIP)
-            near[y * 2 + b, part, :] += far[b, part, :]
+            value = near[y * 2 + b, part, :] + far[b, part, :]
+            near[y * 2 + b, part, :] = value
+            high = value.astype(jnp.bfloat16)
+            spot = pl.ds(pl.multiple_of(b * local_rows + t * STRIP, STRIP), STRIP)
+            m_hi[spot, :] = high
+            m_lo[spot, :] = (value - high.astype(jnp.float32)).astype(jnp.bfloat16)
             return inner
 
         lax.fori_loop(0, local_rows // STRIP, total, 0)
         finish(b).start()
 
-    def drain(k, carry):
-        slot, source_z, partner = place(k)
-        forwards(slot, source_z, partner, lambda copy: copy.wait_send())
-
-        @pl.when(is_root)
-        def _():
-            to_other(slot).wait_send()
-            to_mate(slot).wait_send()
-            keep_own(slot).wait()
-
-        @pl.when(is_relay)
-        def _():
-            relay(slot).wait_send()
-
-        @pl.when(jnp.logical_not(jnp.logical_or(is_root, is_relay)))
-        def _():
-            relay(slot).wait_recv()
-
+    columns = pl.ds(0, width)
+
+    def gram(slot):
+        pltpu.make_async_copy(
+            mr_ref.at[slot], m_buf.at[slot, pl.ds(0, local_rows)], rows_sem.at[slot]).wait()
+
+        def cut(t, inner):
+            part = pl.ds(pl.multiple_of(t * STRIP, STRIP), STRIP)
+            value = m_buf[slot, part, :]
+            high = value.astype(jnp.bfloat16)
+            s_hi[part, columns] = high
+            s_lo[part, columns] = (value - high.astype(jnp.float32)).astype(jnp.bfloat16)
+            return inner
+
+        lax.fori_loop(0, local_rows // STRIP, cut, 0)
+        for b in range(2):
+            sums = None
+            for d in range(local_rows // TILE_ROWS):
+                part = pl.ds(d * TILE_ROWS, TILE_ROWS)
+                spot = pl.ds(b * local_rows + d * TILE_ROWS, TILE_ROWS)
+                u, v = s_hi[part, columns], s_lo[part, columns]
+                a, e = m_hi[spot, :], m_lo[spot, :]
+                term = crossed(u, a) + crossed(u, e) + crossed(v, a)
+                sums = term if sums is None else sums + term
+            m_buf[slot, pl.ds(local_rows + b * width, width), :] = sums
+
+    block = pl.ds(local_rows, 2 * width)
+
+    def over_x(slot, source_z):
+        return pltpu.make_async_remote_copy(
+            src_ref=m_buf.at[slot, block], dst_ref=gram_x.at[source_z],
+            send_sem=x_send.at[source_z], recv_sem=x_recv.at[source_z],
+            device_id=across, device_id_type=MESH)
+
+    def over_z(slot, source_z, spot, target):
+        return pltpu.make_async_remote_copy(
+            src_ref=m_buf.at[slot, block], dst_ref=gram_z.at[spot],
+            send_sem=z_send.at[source_z], recv_sem=z_recv.at[spot],
+            device_id=target, device_id_type=MESH)
+
+    def add_to(slot, ref, spot):
+        def one(t, inner):
+            part = pl.ds(pl.multiple_of(t * STRIP, STRIP), STRIP)
+            here = pl.ds(pl.multiple_of(local_rows + t * STRIP, STRIP), STRIP)
+            m_buf[slot, here, :] += ref[spot, part, :]
+            return inner
+
+        lax.fori_loop(0, 2 * width // STRIP, one, 0)
+
+    stage = local_rows + 4 * width
+
+    def add_staged(slot, spot):
+        copy = pltpu.make_async_copy(
+            gram_z.at[spot], m_buf.at[slot, pl.ds(stage, 2 * width)], stage_sem)
+        copy.start()
+        copy.wait()
+
+        def one(t, inner):
+            part = pl.ds(pl.multiple_of(stage + t * STRIP, STRIP), STRIP)
+            here = pl.ds(pl.multiple_of(local_rows + t * STRIP, STRIP), STRIP)
+            m_buf[slot, here, :] += m_buf[slot, part, :]
+            return inner
+
+        lax.fori_loop(0, 2 * width // STRIP, one, 0)
+
+    def send_x(i, carry):
+        source_z = line(span - 1 - i)
+        slot = source_z * 2 + 1 - x
+        gram(slot)
+        over_x(slot, source_z).start()
         return carry
 
-    lax.fori_loop(0, rows, drain, 0)
+    lax.fori_loop(0, span, send_x, 0)
+
+    def down_spot(source_z):
+        return jnp.where(source_z == z - 1, span, source_z)
+
+    def send_z(i, carry):
+        source_z = line(span - 1 - i)
+        slot = source_z * 2 + x
+        gram(slot)
+        over_x(slot, source_z).wait_recv()
+        add_to(slot, gram_x, source_z)
+
+        @pl.when(jnp.logical_and(source_z >= z, has_below))
+        def _():
+            over_z(slot, source_z, source_z, above).wait_recv()
+            add_staged(slot, source_z)
+
+        @pl.when(jnp.logical_and(source_z <= z, has_above))
+        def _():
+            spot = jnp.where(source_z == z, span, source_z)
+            over_z(slot, source_z, spot, below).wait_recv()
+            add_staged(slot, spot)
+
+        @pl.when(source_z > z)
+        def _():
+            over_z(slot, source_z, source_z, above).start()
+
+        @pl.when(source_z < z)
+        def _():
+            over_z(slot, source_z, down_spot(source_z), below).start()
+
+        return carry
+
+    lax.fori_loop(0, span, send_z, 0)
+
+    def child(b):
+        return pltpu.make_async_copy(
+            p_buf.at[pl.ds(b * width, width)], child_ref.at[:, pl.ds(b * width, width)],
+            child_sem.at[b])
+
+    for b in range(2):
+        pivot(b).wait()
+
+        def subtract(t, inner):
+            part = pl.ds(pl.multiple_of(b * width + t * STRIP, STRIP), STRIP)
+            here = pl.ds(pl.multiple_of(local_rows + b * width + t * STRIP, STRIP), STRIP)
+            base = pl.ds(pl.multiple_of(local_rows + (2 + b) * width + t * STRIP, STRIP), STRIP)
+            p_buf[part, :] = m_buf[0, base, :] - m_buf[r, here, :]
+            return inner
+
+        lax.fori_loop(0, width // STRIP, subtract, 0)
+        child(b).start()
+
+    def settle(i, carry):
+        over_x(i * 2 + 1 - x, i).wait_send()
+
+        @pl.when(i > z)
+        def _():
+            over_z(i * 2 + x, i, i, above).wait_send()
+
+        @pl.when(i < z)
+        def _():
+            over_z(i * 2 + x, i, down_spot(i), below).wait_send()
+
+        return carry
+
+    lax.fori_loop(0, span, settle, 0)
     for b in range(2):
         chip_sum((1 - y) * 4 + core * 2 + b).wait_send()
         finish(b).wait()
+        child(b).wait()
+
+
+def crossed(left, right):
+    return lax.dot_general(
+        left, right, (((0,), (0,)), ((), ())), preferred_element_type=jnp.float32)
 
 
 def fused(separator_inverse, panel, block_rows, pivot_inverse):
@@ -354,36 +571,41 @@
     col_keep = lax.dynamic_slice_in_dim(block_rows, col_index * col_blocks, col_blocks)
     row_keep = lax.dynamic_slice_in_dim(block_rows, row_index * row_blocks, row_blocks)
     col_mask = jnp.repeat(col_keep.astype(jnp.float32), BS)[None, :]
-    row_mask = -jnp.repeat(row_keep.astype(jnp.float32), BS)[:, None]
+    row_mask = -jnp.broadcast_to(
+        row_keep.astype(jnp.float32)[:, None, None], (row_blocks, 1, width))
     dma, f32, bf16 = pltpu.SemaphoreType.DMA, jnp.float32, jnp.bfloat16
     flops = 6 * local_rows * local_cols * rows * width
-    off, source = pl.pallas_call(
+    off, child, _, _ = pl.pallas_call(
         functools.partial(device_kernel, (rows, cols, rows // 2)),
         out_shape=(jax.ShapeDtypeStruct((local_rows, 2 * width), f32),
-                   jax.ShapeDtypeStruct((rows, local_rows, width), f32)),
+                   jax.ShapeDtypeStruct((width, 2 * width), f32),
+                   jax.ShapeDtypeStruct((rows, local_rows, width), f32),
+                   jax.ShapeDtypeStruct((5, 2 * width, width), f32)),
         in_specs=[pl.BlockSpec(memory_space=pl.ANY), pl.BlockSpec(memory_space=pl.ANY),
-                  pl.BlockSpec(memory_space=pltpu.VMEM), pl.BlockSpec(memory_space=pltpu.VMEM)],
-        out_specs=(pl.BlockSpec(memory_space=pl.ANY), pl.BlockSpec(memory_space=pl.ANY)),
+                  pl.BlockSpec(memory_space=pltpu.VMEM), pl.BlockSpec(memory_space=pltpu.VMEM),
+                  pl.BlockSpec(memory_space=pl.ANY)],
+        out_specs=(pl.BlockSpec(memory_space=pl.ANY),) * 4,
         scratch_shapes=[
             pltpu.VMEM((local_rows, local_cols), bf16),
             pltpu.VMEM((local_rows, local_cols), bf16),
             pltpu.VMEM((rows, local_cols, width), f32),
             pltpu.VMEM((local_cols, width), bf16),
             pltpu.VMEM((local_cols, width), bf16),
-            pltpu.VMEM((2, local_rows, width), f32),
+            pltpu.VMEM((local_rows, width), f32),
             pltpu.VMEM((4, local_rows, width), f32),
             pltpu.VMEM((2, local_rows, width), f32),
-            dma((2,)), dma, dma((3, rows)), dma((rows,)), dma, dma((4,)),
-            dma((2,)), dma((2,)), dma((2, rows)), dma((rows,)), dma((rows,)), dma((2,)),
+            pltpu.VMEM((4, 2 * width, width), f32),
+            dma((2,)), dma, dma((3, rows)), dma((rows,)), dma((3, rows)), dma((rows,)),
+            dma, dma((4,)), dma((2,)), dma((2,)), dma((2, rows)), dma((rows,)), dma((rows,)),
+            dma((2,)), dma((rows,)), dma((4,)), dma((4,)), dma((4,)), dma((5,)), dma((2,)),
+            dma((2,)), dma,
         ],
         compiler_params=pltpu.CompilerParams(
             collective_id=0, has_side_effects=True, vmem_limit_bytes=VMEM_BYTES),
         cost_estimate=pl.CostEstimate(
             flops=flops, bytes_accessed=4 * local_rows * local_cols, transcendentals=0),
-    )(separator_inverse, panel, col_mask, row_mask)
-    gram_part = product(source, off, ((1,), (0,))).reshape(rows * width, 2 * width)
-    gram_share = lax.psum_scatter(gram_part, "prow", scatter_dimension=0, tiled=True)
-    return (off, pivot_inverse - gram_share)
+    )(separator_inverse, panel, col_mask, row_mask, pivot_inverse)
+    return (off, child)
 
 
 def solution(mesh):

time: 460 us -> 404 us (0.88)
  waiting for transfers between devices: 102 us -> 0 us
  Pallas kernels: 321 us -> 395 us
  matrix products: 15.3 us -> 0 us
  between operations: 14 us -> 0.65 us
    reduce_scatter x1 -> x0, waiting for transfers between devices: 102 us -> none  [fused(): lax.psum_scatter(gram_part, 'prow', scatter_dimension=0, tiled=True)]
    pallas_call x1, Pallas kernels: 321 us -> 395 us  [fused(): pl.pallas_call(functools.partial(device_kernel, (rows, cols, rows // 2)),...]
    dot_general x1 -> x0, matrix products: 15.3 us -> none  [product(): lax.dot_general(left, right, (dims, ((), ())), precision=lax.Precision.HI...]
  transfers between devices with their start and end apart: 1 -> 0, of which waited for: 1 -> 0; matrix products, arithmetic and copies ran while one was open for 0% -> 0% of each run, Pallas kernels for 0% -> 0%
where the time goes in v2:
time: 404 us; the launch traced here: 403 us
  Pallas kernels  395 us (98%)
  local copies, waits for them, and re-layouts  6.04 us (1%)
    pallas_call x1, Pallas kernels, fused(): pl.pallas_call(functools.partial(device_kernel, (rows, cols, rows // 2)),...  395 us

profile of v2, /device:TPU:0, one launch (start us, length us, event | category | flops | bytes accessed | tf_op | source)
XLA Modules:
  0.0 403.4 jit_solution(15797395274086056251)
XLA Ops:
  0.6 0.7 convert_negate_fusion
  1.4 0.7 dynamic-slice_convert_fusion
  2.1 0.6 broadcast_in_dim.10.rowmask_ref
  2.7 0.1 broadcast_bitcast_fusion
  2.8 0.6 copy.6
  3.4 395.3 %shard_map.59 = (f32[1536,512]{1,0:T(8,128)}, f32[256,512]{1,0:T(8,128)}, f32[8,1536,256]{2,1,0:T(8,128)}, f32[5,512,256]{2,1,0:T(8,128)}) custom-call(f32[1536,3072]{1,0:T(8,128)} %sep_ref.1, f32[3072,256]{1,0:T(8,128)} %panel_ref.1, f32[1,3072]{1,0:T(1,128)} %bitcast.4, f32[2,1,256]{2,1,0:T(1,128)} %broadcast_in_dim.10.rowmask_ref, f32[256,512]{1,0:T(8,128)} %pivot_ref.1), custom_call_target="tpu_custom_call" | custom-call | flops 57982058496 | bytes 18874368 | tf_op jit(solution)/shard_map/pallas_call | solution.py:578
  398.7 0.0 copy-start
  398.7 3.9 copy.9
  402.6 0.0 copy-done
  402.6 0.8 copy.10
Async XLA Ops:
  398.7 3.9 copy-start

commit v3 on v2

--- a/solution.py
+++ b/solution.py
@@ -80,7 +80,7 @@
 def device_kernel(geometry, sep_ref, panel_ref, colmask_ref, rowmask_ref, pivot_ref,
                   off_ref, child_ref, mr_ref, gram_z,
                   s_hi, s_lo, m_buf, m_hi, m_lo, p_buf, near, far, gram_x,
-                  load_sem, own_sem, gather_send, gather_recv, late_send, late_recv,
+                  load_sem, own_sem, gather_send, gather_recv, second_send, second_recv, late_send, late_recv,
                   p_send, near_recv, far_send, far_recv, root_send, root_recv, root_own, out_sem,
                   rows_sem, x_send, x_recv, z_send, z_recv, pivot_sem, child_sem, stage_sem):
     rows, cols, span = geometry
@@ -136,12 +136,19 @@
         return source_z * 2 + jnp.where(partner, 1 - x, x), source_z, partner
 
     def gather(slot, way, target):
-        part = pl.ds(0, EARLY)
+        part = pl.ds(0, EARLY // 2)
         return pltpu.make_async_remote_copy(
             src_ref=m_buf.at[slot, part], dst_ref=m_buf.at[slot, part],
             send_sem=gather_send.at[way, slot], recv_sem=gather_recv.at[slot],
             device_id=target, device_id_type=MESH)
 
+    def gather_second(slot, way, target):
+        part = pl.ds(EARLY // 2, EARLY // 2)
+        return pltpu.make_async_remote_copy(
+            src_ref=m_buf.at[slot, part], dst_ref=m_buf.at[slot, part],
+            send_sem=second_send.at[way, slot], recv_sem=second_recv.at[slot],
+            device_id=target, device_id_type=MESH)
+
     def gather_late(slot, way, target):
         part = pl.ds(EARLY, local_cols - EARLY)
         return pltpu.make_async_remote_copy(
@@ -164,16 +171,39 @@
         def _():
             act(copy(slot, 2, below))
 
-    def forwards(slot, source_z, partner, act):
-        @pl.when(jnp.logical_not(partner))
-        def _():
-            @pl.when(source_z == z)
-            def _():
-                act(gather_late(slot, 0, across))
-
-            along(gather_late, slot, source_z, act)
-            along(gather, slot, source_z, act)
-            act(gather(slot, 0, across))
+    def first_half(slot, source_z, act):
+        along(gather, slot, source_z, act)
+        act(gather(slot, 0, across))
+
+    def second_half(slot, source_z, act):
+        @pl.when(source_z == z)
+        def _():
+            act(gather_late(slot, 0, across))
+
+        along(gather_late, slot, source_z, act)
+        along(gather_second, slot, source_z, act)
+        act(gather_second(slot, 0, across))
+
+    def begin(j):
+        source_z = line(j)
+        slot = source_z * 2 + x
+        gather(slot, 0, across).wait_recv()
+        first_half(slot, source_z, lambda copy: copy.start())
+
+    def complete(j):
+        source_z = line(j)
+        slot = source_z * 2 + x
+        gather_late(slot, 0, across).wait_recv()
+        gather_second(slot, 0, across).wait_recv()
+        second_half(slot, source_z, lambda copy: copy.start())
+
+    inner = jnp.logical_and(has_above, has_below)
+    outer = jnp.logical_not(inner)
+
+    def at(now, turn, who, act, j):
+        @pl.when(jnp.logical_and(now == turn, who))
+        def _():
+            act(j)
 
     def passes_on(source_z):
         return jnp.logical_or(goes_up(source_z), goes_down(source_z))
@@ -227,7 +257,8 @@
         return lax.rem(slot // 2, 2)
 
     own.wait()
-    forwards(r, z, jnp.bool_(False), lambda copy: copy.start())
+    first_half(r, z, lambda copy: copy.start())
+    second_half(r, z, lambda copy: copy.start())
 
     tiles = 2 * (local_cols // width)
 
@@ -262,15 +293,20 @@
     def step(k, carry):
         slot, source_z, partner = place(k)
 
-        @pl.when(k > 0)
+        at(k, 1, True, complete, 1)
+        at(k, 1, inner, complete, 2)
+        at(k, 3, outer, complete, 2)
+        at(k, 4, inner, complete, 3)
+        at(k, 5, outer, complete, 3)
+
+        @pl.when(partner)
         def _():
             gather(slot, 0, across).wait_recv()
-
-            @pl.when(jnp.logical_not(jnp.logical_and(partner, passes_on(source_z))))
+            gather_second(slot, 0, across).wait_recv()
+
+            @pl.when(jnp.logical_not(passes_on(source_z)))
             def _():
                 gather_late(slot, 0, across).wait_recv()
-
-            forwards(slot, source_z, partner, lambda copy: copy.start())
 
         for turn, j in ((1, 0), (3, 1), (5, 2), (5, 3)):
             @pl.when(k == turn)
@@ -321,6 +357,12 @@
         def _():
             partial(slot).start()
 
+        at(k, 0, True, begin, 1)
+        at(k, 0, inner, begin, 2)
+        at(k, 2, outer, begin, 2)
+        at(k, 3, inner, begin, 3)
+        at(k, 4, outer, begin, 3)
+
         @pl.when(k > 0)
         def _():
             relay_at(k - 1)
@@ -360,7 +402,11 @@
 
     def drain(k, carry):
         slot, source_z, partner = place(k)
-        forwards(slot, source_z, partner, lambda copy: copy.wait_send())
+
+        @pl.when(jnp.logical_not(partner))
+        def _():
+            first_half(slot, source_z, lambda copy: copy.wait_send())
+            second_half(slot, source_z, lambda copy: copy.wait_send())
 
         @pl.when(partner)
         def _():
@@ -596,6 +642,7 @@
             pltpu.VMEM((2, local_rows, width), f32),
             pltpu.VMEM((4, 2 * width, width), f32),
             dma((2,)), dma, dma((3, rows)), dma((rows,)), dma((3, rows)), dma((rows,)),
+            dma((3, rows)), dma((rows,)),
             dma, dma((4,)), dma((2,)), dma((2,)), dma((2, rows)), dma((rows,)), dma((rows,)),
             dma((2,)), dma((rows,)), dma((4,)), dma((4,)), dma((4,)), dma((5,)), dma((2,)),
             dma((2,)), dma,

time: 404 us -> 396 us (0.980)
  Pallas kernels: 395 us -> 386 us
    pallas_call x1, Pallas kernels: 395 us -> 386 us  [fused(): pl.pallas_call(functools.partial(device_kernel, (rows, cols, rows // 2)),...]
where the time goes in v3:
time: 396 us; the launch traced here: 394 us
  Pallas kernels  386 us (97%)
  local copies, waits for them, and re-layouts  6.04 us (2%)
    pallas_call x1, Pallas kernels, fused(): pl.pallas_call(functools.partial(device_kernel, (rows, cols, rows // 2)),...  386 us

profile of v3, /device:TPU:0, one launch (start us, length us, event | category | flops | bytes accessed | tf_op | source)
XLA Modules:
  0.0 394.1 jit_solution(11579297505524789838)
XLA Ops:
  0.6 0.7 convert_negate_fusion
  1.4 0.7 dynamic-slice_convert_fusion
  2.1 0.6 broadcast_in_dim.10.rowmask_ref
  2.7 0.1 broadcast_bitcast_fusion
  2.8 0.6 copy.6
  3.4 386.0 %shard_map.59 = (f32[1536,512]{1,0:T(8,128)}, f32[256,512]{1,0:T(8,128)}, f32[8,1536,256]{2,1,0:T(8,128)}, f32[5,512,256]{2,1,0:T(8,128)}) custom-call(f32[1536,3072]{1,0:T(8,128)} %sep_ref.1, f32[3072,256]{1,0:T(8,128)} %panel_ref.1, f32[1,3072]{1,0:T(1,128)} %bitcast.4, f32[2,1,256]{2,1,0:T(1,128)} %broadcast_in_dim.10.rowmask_ref, f32[256,512]{1,0:T(8,128)} %pivot_ref.1), custom_call_target="tpu_custom_call" | custom-call | flops 57982058496 | bytes 18874368 | tf_op jit(solution)/shard_map/pallas_call | solution.py:624
  389.4 0.0 copy-start
  389.4 3.9 copy.9
  393.3 0.0 copy-done
  393.3 0.8 copy.10
Async XLA Ops:
  389.4 3.9 copy-start
